TPU v7x, 256 devices: a whole 4x4x8 slice. The times are simulated.
256 devices in a mesh: gz: 64 (over x, y_lo, z), col: 2 (over core), af: 2 (over y_hi).
Axes of the slice: x: 4, y: 4 (y_hi: 2, y_lo: 2; y = y_hi * 2 + y_lo), z: 8, core: 2. Of those that a mesh axis runs over, the one named last changes fastest.
Arguments:
- volume: bfloat16 [128, 24, 24, 512], P('gz', 'af', None, 'col'), may hold values from -6 to 6
- kernel: bfloat16 [3, 3, 3, 512, 512], P(None, None, None, 'col', 'af'), may hold values from -0.0546875 to 0.0546875
- out_grad: bfloat16 [64, 12, 12, 512], P('gz', 'col', None, 'af'), may hold values from -6 to 6
Outputs:
- output: bfloat16 [64, 12, 12, 512], P('gz', 'col', None, 'af')
- volume_grad: bfloat16 [128, 24, 24, 512], P('gz', 'af', None, 'col')
- kernel_grad: bfloat16 [3, 3, 3, 512, 512], P(None, None, None, 'col', 'af')
All inputs are finite; a program needn't handle non-finite values.
Results may differ from a plain program's by a relative error of at most 0.013.
Values may be sent and summed in bfloat16 or wider, within the bound.
A program may use at most 128 MiB of HBM per device.

v0:
```python
import jax
import jax.numpy as jnp
from jax import lax
from jax.sharding import PartitionSpec as P


def from_behind(value, axis, steps):
    count = lax.axis_size(axis)
    initial, last = (max(0, -steps), min(count, count - steps))
    return lax.ppermute(value, axis, [(source, source + steps) for source in range(initial, last)])


def tap_slice(padded, dz, dx, dy, planes, rows):
    limit = (dz + 2 * planes - 1, dx + 2 * rows - 1, dy + 2 * rows - 1, padded.shape[3])
    return lax.slice(padded, (dz, dx, dy, 0), limit, (2, 2, 2, 1))


def placed_term(contrib, dz, dx, dy):
    if dz == 2:
        contrib = jnp.pad(contrib, ((1, 0), (0, 0), (0, 0), (0, 0)))
    else:
        contrib = jnp.pad(contrib, ((0, 1), (0, 0), (0, 0), (0, 0)))
    if dx == 0:
        contrib = jnp.pad(contrib[:, 1:], ((0, 0), (0, 1), (0, 0), (0, 0)))
    if dy == 0:
        contrib = jnp.pad(contrib[:, :, 1:], ((0, 0), (0, 0), (0, 1), (0, 0)))
    return contrib


def on_device(volume, kernel, out_grad):
    planes = out_grad.shape[0]
    top_plane = volume[-1:]
    below = from_behind(top_plane, "gz", 1)
    framed = jnp.concatenate([below, volume], 0)
    whole = lax.all_gather(framed, "af", axis=1, tiled=True)
    rows = whole.shape[1] // 2
    padded = jnp.pad(whole, ((0, 0), (1, 0), (1, 0), (0, 0)))
    filters = kernel.shape[4]
    channels = kernel.shape[3]
    partial_value = jnp.zeros((planes, rows, rows, filters), jnp.float32)
    for dz in range(3):
        for dx in range(3):
            for dy in range(3):
                piece = tap_slice(padded, dz, dx, dy, planes, rows)
                partial_value = partial_value + jnp.einsum(
                    "zxyc,cf->zxyf", piece, kernel[dz, dx, dy], preferred_element_type=jnp.float32
                )
    output = lax.psum_scatter(
        partial_value.astype(jnp.bfloat16), "col", scatter_dimension=1, tiled=True
    )
    grad_full = lax.all_gather(out_grad, "col", axis=1, tiled=True)
    blocks = {}
    weight_terms = []
    for dz in range(3):
        for dx in range(3):
            for dy in range(3):
                contrib = jnp.einsum(
                    "zxyf,cf->zxyc",
                    grad_full,
                    kernel[dz, dx, dy],
                    preferred_element_type=jnp.float32,
                )
                parity_key = (dz % 2, 0 if dx == 1 else 1, 0 if dy == 1 else 1)
                placed = placed_term(contrib, dz, dx, dy)
                if parity_key in blocks:
                    blocks[parity_key] = blocks[parity_key] + placed
                else:
                    blocks[parity_key] = placed
                piece = tap_slice(padded, dz, dx, dy, planes, rows)
                weight_terms.append(
                    jnp.einsum(
                        "zxyc,zxyf->cf", piece, grad_full, preferred_element_type=jnp.float32
                    )
                )
    z_layers = []
    for z_parity in range(2):
        x_layers = []
        for x_parity in range(2):
            x_layers.append(
                jnp.stack([blocks[z_parity, x_parity, 0], blocks[z_parity, x_parity, 1]], 3)
            )
        z_layers.append(jnp.stack(x_layers, 2))
    joined = jnp.stack(z_layers, 1)
    framed_grad = joined.reshape(2 * planes + 2, 2 * rows, 2 * rows, channels)[: 2 * planes + 1]
    arrived = from_behind(framed_grad[0:1].astype(jnp.bfloat16), "gz", -1).astype(jnp.float32)
    owned = framed_grad[1:]
    owned = jnp.concatenate([owned[:-1], owned[-1:] + arrived], 0)
    volume_grad = lax.psum_scatter(
        owned.astype(jnp.bfloat16), "af", scatter_dimension=1, tiled=True
    )
    weight_local = jnp.stack(weight_terms, 0)
    scale = 1.0 / jnp.sqrt(jnp.float32(planes * lax.axis_size("gz") * rows * rows))
    weight_sum = lax.psum(weight_local, "gz")
    kernel_grad = (weight_sum * scale).astype(jnp.bfloat16).reshape(3, 3, 3, channels, filters)
    return (output, volume_grad, kernel_grad)


def solution(mesh):
    in_specs = (
        P("gz", "af", None, "col"),
        P(None, None, None, "col", "af"),
        P("gz", "col", None, "af"),
    )
    out_specs = (
        P("gz", "col", None, "af"),
        P("gz", "af", None, "col"),
        P(None, None, None, "col", "af"),
    )
    return jax.shard_map(
        on_device, mesh=mesh, in_specs=in_specs, out_specs=out_specs, check_vma=False
    )
```

profile of v0, /device:TPU:8, one launch (start us, length us, event | category | flops | bytes accessed | tf_op | source)
XLA Modules:
  0.0 797.9 jit_solution(7340381981078000997)
XLA Ops:
  9.1 4.0 collective-permute-start
  13.1 2.1 all_gather.7
  15.2 1.1 convolution_bitcast_fusion.52
  16.3 1.1 convolution_bitcast_fusion.51
  17.4 1.1 convolution_bitcast_fusion.50
  18.5 1.1 convolution_bitcast_fusion.49
  19.6 1.1 convolution_bitcast_fusion.48
  20.8 1.1 convolution_bitcast_fusion.47
  21.9 1.1 convolution_bitcast_fusion.46
  23.0 1.1 convolution_bitcast_fusion.45
  30.8 3.6 copy.8
  34.5 3.1 reshape.285
  38.5 5.7 collective-permute-start.1
  44.3 14.1 %all_gather.6 = bf16[3,24,24,256]{3,2,1,0:T(8,128)(2,1)S(1)} all-gather(bf16[3,12,24,256]{3,2,1,0:T(8,128)(2,1)S(1)} %pad_maximum_fusion.2), channel_id=1, replica_groups=mesh['gz'=64,'col'=2,'af'=2] {'af'}, dimensions={1}, use_global_device_ids=true | all-gather | bytes 1327104 | tf_op jit(solution)/shard_map/all_gather | solution.py:35
  66.6 3.7 slice.324
  70.3 3.7 slice.322
  74.0 3.7 slice.320
  77.7 3.7 slice.318
  81.4 1.8 fusion.26
  83.3 1.8 fusion.25
  85.1 1.8 fusion.24
  106.8 3.8 slice.366
  110.5 3.7 slice.364
  114.2 1.9 fusion.3
  116.1 1.2 fusion.29
  123.0 1.2 fusion.63
  124.2 1.1 convolution_add_fusion.25
  131.9 1.1 convolution_add_fusion.18
  139.7 24.3 %all-reduce.52.cloned.1.call-done = bf16[2,24,24,256]{3,2,1,0:T(8,128)(2,1)} async-done(((bf16[2,24,24,256]{3,2,1,0:T(8,128)(2,1)}), bf16[2,24,24,256]{3,2,1,0:T(8,128)(2,1)}) %all-reduce.52.cloned.1.call-update) | async-done | bytes 589840
  164.0 1.7 constant_dynamic-slice_fusion
  165.7 619.0 %all-reduce.50.cloned.1.call-done = f32[27,256,256]{2,1,0:T(8,128)} async-done(((f32[27,256,256]{2,1,0:T(8,128)}), f32[27,256,256]{2,1,0:T(8,128)}) %all-reduce.50.cloned.1.call-update) | async-done | bytes 7077904 | tf_op jit(solution)/shard_map/psum | solution.py:93
  784.7 5.7 multiply_convert_fusion
  (161 shorter events, 54.5 us)
Async XLA Ops:
  8.0 156.0 %all-reduce.52.cloned.1.call-start = ((), (), s32[]{:S(2)}) async-start(), calls=%async_computation.3 | async-start | bytes 1179648
  8.0 16.1 %copy-start = (bf16[3,3,3,256,256]{4,3,2,1,0:T(8,128)(2,1)S(1)}, bf16[3,3,3,256,256]{4,3,2,1,0:T(8,128)(2,1)}, u32[]{:S(2)}) copy-start(bf16[3,3,3,256,256]{4,3,2,1,0:T(8,128)(2,1)} %param.4) | copy-start | bytes 10616836
  9.1 35.1 %collective-permute-start = (bf16[1,12,24,256]{3,2,1,0:T(8,128)(2,1)S(1)}, bf16[1,12,24,256]{3,2,1,0:T(8,128)(2,1)S(1)}, u32[]{:S(2)}, u32[]{:S(2)}) collective-permute-start(bf16[1,12,24,256]{3,2,1,0:T(8,128)(2,1)S(1)} %slice.317), channel_id=1, source_target_pairs={{0,4},{4,8},{8,12},{12,16},{16,20},{20,24},{24,28},{28,32},{32,36}... | collective-permute-start | bytes 442376 | tf_op jit(solution)/shard_map/ppermute | solution.py:10
  37.6 6.7 copy-start.2
  37.6 6.6 copy-start.3
  38.5 77.6 %collective-permute-start.1 = (bf16[1,24,24,256]{3,2,1,0:T(8,128)(2,1)}, bf16[1,24,24,256]{3,2,1,0:T(8,128)(2,1)}, u32[]{:S(2)}, u32[]{:S(2)}) collective-permute-start(bf16[1,24,24,256]{3,2,1,0:T(8,128)(2,1)} %get-tuple-element.4), channel_id=1, source_target_pairs={{4,0},{8,4},{12,8},{16,12},{20,16},{24,20},{28,24},{32,28},{36,32}... | collective-permute-start | bytes 884744 | tf_op jit(solution)/shard_map/ppermute | solution.py:10
  66.2 22.6 %copy-start.5 = (bf16[1,12,12,256]{3,2,1,0:T(8,128)(2,1)}, bf16[1,12,12,256]{3,2,1,0:T(8,128)(2,1)S(1)}, u32[]{:S(2)}) copy-start(bf16[1,12,12,256]{3,2,1,0:T(8,128)(2,1)S(1)} %slice.328) | copy-start | bytes 221188
  66.6 22.3 %copy-start.8 = (bf16[1,12,12,256]{3,2,1,0:T(8,128)(2,1)}, bf16[1,12,12,256]{3,2,1,0:T(8,128)(2,1)S(1)}, u32[]{:S(2)}) copy-start(bf16[1,12,12,256]{3,2,1,0:T(8,128)(2,1)S(1)} %slice.326) | copy-start | bytes 221188
  81.4 5.5 copy-start.10
  114.2 4.0 copy-start.4
  118.2 666.5 %all-reduce.50.cloned.1.call-start = ((), (), s32[]{:S(2)}) async-start(), calls=%async_computation.2 | async-start | bytes 14155776 | tf_op jit(solution)/shard_map/psum | solution.py:93
  121.1 0.7 copy-start.15
  121.1 1.9 copy-start.14
  121.1 3.2 copy-start.13
  121.1 4.3 copy-start.12
  121.1 5.3 copy-start.11
  121.1 6.4 copy-start.9
  121.1 7.5 copy-start.6
  121.1 669.3 %reduce-scatter.5.cloned.1.call-start = ((), (), s32[]{:S(2)}) async-start(), calls=%async_computation.1 | async-start | bytes 147456 | tf_op jit(solution)/shard_map/reduce_scatter | solution.py:48
  123.0 13.3 %copy-start.1 = (bf16[3,3,3,256,256]{4,3,2,1,0:T(8,128)(2,1)S(1)}, bf16[3,3,3,256,256]{4,3,2,1,0:T(8,128)(2,1)}, u32[]{:S(2)}) copy-start(bf16[3,3,3,256,256]{4,3,2,1,0:T(8,128)(2,1)} %param.4) | copy-start | bytes 10616836
  136.3 2.0 copy-start.7
Sparse Core Ops, SparseCore 0:
  118.3 45.6 all-reduce.51
  166.9 617.7 all-reduce.49
Sparse Core Ops, SparseCore 1:
  139.8 15.9 reduce-scatter.4
where the time goes:
time: 812 us; the launch traced here: 798 us
  waiting for transfers between devices  643 us (79%)
  matrix products  58.6 us (7%)
  local copies, waits for them, and re-layouts  43.2 us (5%)
  between operations  16.8 us (2%)
  blocking collectives  16.2 us (2%)
  starting transfers between devices  9.98 us (1%)
  other arithmetic  9.71 us (1%)
    psum x1, waiting for transfers between devices, on_device(): weight_sum = lax.psum(weight_local, 'gz')  619 us
    slice x27, local copies, waits for them, and re-layouts, tap_slice(): return lax.slice(padded, (dz, dx, dy, 0), limit, (2, 2, 2, 1))  30.6 us
    dot_general x27, matrix products, on_device(): jnp.einsum('zxyc,zxyf->cf', piece, grad_full, preferred_element_type=jnp....  29 us
    unnamed x4, waiting for transfers between devices  24.3 us
    dot_general x27, matrix products, on_device(): jnp.einsum('zxyc,cf->zxyf', piece, kernel[dz, dx, dy], preferred_element_...  16.6 us
  transfers between devices with their start and end apart: 5, of which 2 were waited for; matrix products, arithmetic and copies ran while one was open for 14% of the time, Pallas kernels for 0%

commit v1 on v0

v1 whole, which is shorter than its diff:
```python
import functools

import jax
import jax.numpy as jnp
from jax import lax
from jax.experimental import pallas as pl
from jax.experimental.pallas import tpu as pltpu
from jax.sharding import PartitionSpec as P

F32 = jnp.float32
BF16 = jnp.bfloat16
MESH = pl.DeviceIdType.MESH
NX, NY, NZ = 4, 2, 8
SHARD = 112
YZ = NY * NZ
BLOCK = SHARD * YZ
ROWS = BLOCK * NX
TAP_ROWS = 27 * 256


def rows_of(start, size):
    return pl.ds(pl.multiple_of(start, 16), size)


def body(
    v, k, og, out, vg, kg,
    k3, og3, vs, vin, halo, acc, vacc, oin, osend, vg_af, vg_gz, vin_af, vin_gz,
    ws, rx, s2, ry, full,
    local_sem, es, er, xs, xr, ys, yr, gs, gr, hs, hr,
):
    gz, col, af = lax.axis_index("gz"), lax.axis_index("col"), lax.axis_index("af")
    count = NX * YZ
    x, y, z = gz // YZ, (gz // NZ) % NY, gz % NZ
    up, down = lax.rem(gz + 1, count), lax.rem(gz + count - 1, count)

    def dev(g, c=col, a=af):
        return {"gz": g, "col": c, "af": a}

    def x_peer(d):
        return lax.rem(x + d, NX)

    def yz_peer(t):
        return lax.rem(y + t // NZ, NY) * NZ + lax.rem(z + t % NZ, NZ)

    def remote(src, dst, ss, rs, target):
        return pltpu.make_async_remote_copy(
            src_ref=src, dst_ref=dst, send_sem=ss, recv_sem=rs, device_id=target, device_id_type=MESH
        )

    barrier = pltpu.get_barrier_semaphore()

    def greet(target):
        pl.semaphore_signal(barrier, inc=1, device_id=target, device_id_type=MESH)

    greet(dev(gz, c=1 - col))
    greet(dev(gz, a=1 - af))
    for g in (up, down):
        greet(dev(g))
        greet(dev(g, a=1 - af))
    for d in range(1, NX):
        greet(dev(x_peer(d) * YZ + y * NZ + z))

    @pl.loop(1, YZ)
    def _(t):
        greet(dev(x * YZ + yz_peer(t)))

    loads = [
        pltpu.make_async_copy(k.at[:, c], k3.at[:, :, pl.ds(c * 256, 256)], local_sem.at[c])
        for c in range(3)
    ]
    for load in loads:
        load.start()

    og3[pl.ds(12, 1)] = jnp.zeros((1, 32, 768), BF16)
    og3[pl.ds(6 * col, 6)] = og[...]
    vs[...] = jnp.zeros(vs.shape, BF16)
    ws[pl.ds(TAP_ROWS, ROWS - TAP_ROWS)] = jnp.zeros((ROWS - TAP_ROWS, 256), BF16)
    pl.semaphore_wait(barrier, 1 + 1 + 4 + (NX - 1) + (YZ - 1))

    mine = pl.ds(6 * col, 6)
    cot = remote(og, og3.at[mine], es.at[0], er.at[0], dev(gz, c=1 - col))
    to_af = remote(v, vin, es.at[1], er.at[1], dev(gz, a=1 - af))
    top_own = remote(v.at[1], halo.at[0], es.at[2], er.at[2], dev(up))
    top_other = remote(v.at[1], halo.at[1], es.at[3], er.at[3], dev(up, a=1 - af))
    for copy in (cot, to_af, top_other, top_own):
        copy.start()

    own_pairs = pl.ds(1 + 6 * af, 6)
    other_pairs = pl.ds(7 - 6 * af, 6)
    for p in range(2):
        vs[p + 1, own_pairs, :, pl.ds(0, 24)] = v[p]

    for load in loads:
        load.wait()
    cot.wait()

    nt = (((1,), (1,)), ((), ()))

    @pl.loop(0, 3)
    def _(a):
        low = og3[pl.ds(0, 12)].reshape(384, 768)
        high = og3[pl.ds(1, 12)].reshape(384, 768)
        even = lax.dot_general(low, k3[a * 3 + 1], nt, preferred_element_type=F32)
        vacc[a, :, 0] = even.reshape(12, 32, 256)
        odd = lax.dot_general(low, k3[a * 3 + 2], nt, preferred_element_type=F32)
        odd = odd + lax.dot_general(high, k3[a * 3], nt, preferred_element_type=F32)
        vacc[a, :, 1] = odd.reshape(12, 32, 256)

    for p in range(2):
        vg_af[p] = vacc[p + 1, pl.ds(6 - 6 * af, 6), :, pl.ds(0, 24)].astype(BF16)
    vg_gz[0] = vacc[0, pl.ds(6 * af, 6), :, pl.ds(0, 24)].astype(BF16)
    vg_gz[1] = vacc[0, pl.ds(6 - 6 * af, 6), :, pl.ds(0, 24)].astype(BF16)
    back_af = remote(vg_af, vin_af, es.at[4], er.at[4], dev(gz, a=1 - af))
    back_own = remote(vg_gz.at[0], vin_gz.at[0], es.at[5], er.at[5], dev(down))
    back_other = remote(vg_gz.at[1], vin_gz.at[1], es.at[6], er.at[6], dev(down, a=1 - af))
    for copy in (back_af, back_own, back_other):
        copy.start()

    to_af.wait()
    for p in range(2):
        vs[p + 1, other_pairs, :, pl.ds(0, 24)] = vin[p]
    top_own.wait()
    top_other.wait()
    keep = jnp.where(gz > 0, 1.0, 0.0).astype(BF16)
    vs[0, own_pairs, :, pl.ds(0, 24)] = halo[0] * keep
    vs[0, other_pairs, :, pl.ds(0, 24)] = halo[1] * keep

    def planes(a, b):
        start, parity = (0, 1) if b == 0 else (1, b - 1)
        return vs[a, pl.ds(start, 12), parity].reshape(384, 256)

    tn = (((0,), (0,)), ((), ()))

    @pl.loop(0, 3)
    def _(a):
        field = og3[pl.ds(0, 12)].reshape(384, 768)
        for b in range(3):
            grad = lax.dot_general(planes(a, b), field, tn, preferred_element_type=F32).astype(BF16)
            for c in range(3):
                ws[rows_of((a * 9 + b * 3 + c) * 256, 256)] = grad[:, c * 256 : (c + 1) * 256]

    def x_send(d):
        target = x_peer(d)
        return remote(
            ws.at[rows_of(target * BLOCK, BLOCK)], rx.at[d - 1], xs.at[d - 1], xr.at[d - 1],
            dev(target * YZ + y * NZ + z),
        )

    for d in (2, 1, 3):
        x_send(d).start()

    acc[...] = jnp.zeros(acc.shape, F32)

    @pl.loop(0, 3)
    def _(a):
        for b in range(3):
            term = jnp.dot(planes(a, b), k3[a * 3 + b], preferred_element_type=F32)
            for n in range(6):
                acc[n, pl.ds(8, 384)] += term[:, n * 128 : (n + 1) * 128]

    def half(base):
        start = pl.multiple_of(base * 192, 8)
        total = None
        for c in range(3):
            term = jnp.concatenate(
                [
                    acc[c * 2 + lane, pl.ds(7 + c + start, 96, stride=2)]
                    for lane in range(2)
                ],
                axis=1,
            )
            if c == 0:
                place = lax.broadcasted_iota(jnp.int32, (96, 256), 0)
                term = jnp.where(place % 16 == 0, 0.0, term)
            total = term if total is None else total + term
        return total

    osend[...] = half(1 - col).astype(BF16).reshape(6, 16, 256)
    across = remote(osend, oin, es.at[7], er.at[7], dev(gz, c=1 - col))
    across.start()
    own_half = half(col)
    across.wait()
    out[...] = (own_half + oin[...].reshape(96, 256).astype(F32)).astype(BF16).reshape(6, 16, 256)

    for d in (1, 3, 2):
        x_send(d).wait()

    def y_send(t):
        peer = yz_peer(t)
        return remote(
            s2.at[rows_of(peer * SHARD, SHARD)], ry.at[t - 1], ys.at[t - 1], yr.at[t - 1],
            dev(x * YZ + peer),
        )

    def add_block(peer):
        local = rows_of(peer * SHARD, SHARD)
        total = ws[rows_of(x * BLOCK + peer * SHARD, SHARD)].astype(F32)
        for d in range(NX - 1):
            total = total + rx[d, local].astype(F32)
        return total

    @pl.loop(1, YZ)
    def _(t):
        peer = yz_peer(t)
        s2[rows_of(peer * SHARD, SHARD)] = add_block(peer).astype(BF16)
        y_send(t).start()

    back_af.wait()
    back_own.wait()
    back_other.wait()
    own = pl.ds(6 * af, 6)
    vg[0] = (vacc[1, own, :, pl.ds(0, 24)] + vin_af[0].astype(F32)).astype(BF16)
    above = vin_gz[0].astype(F32) + vin_gz[1].astype(F32)
    above = jnp.where(gz < count - 1, above, 0.0)
    vg[1] = (vacc[2, own, :, pl.ds(0, 24)] + vin_af[1].astype(F32) + above).astype(BF16)

    me = y * NZ + z
    for t in range(1, YZ):
        y_send(t).wait()
    total = add_block(me)
    for t in range(1, YZ):
        total = total + ry[t - 1].astype(F32)
    shard = x * BLOCK + me * SHARD
    full[rows_of(shard, SHARD)] = (total * (1.0 / jnp.sqrt(F32(9216)))).astype(BF16)

    def g_send(t):
        place = full.at[rows_of(shard, SHARD)]
        return remote(place, place, gs.at[t - 1], gr.at[t - 1], dev(x * YZ + yz_peer(t)))

    def g_wait(t):
        peer = lax.rem(y + NY - t // NZ, NY) * NZ + lax.rem(z + NZ - t % NZ, NZ)
        place = full.at[rows_of(x * BLOCK + peer * SHARD, SHARD)]
        remote(place, place, gs.at[t - 1], gr.at[t - 1], dev(x * YZ + peer)).wait_recv()

    def h_send(d):
        place = full.at[rows_of(x * BLOCK, BLOCK)]
        return remote(place, place, hs.at[d - 1], hr.at[d - 1], dev(x_peer(d) * YZ + me))

    def h_wait(d):
        source = lax.rem(x + NX - d, NX)
        place = full.at[rows_of(source * BLOCK, BLOCK)]
        remote(place, place, hs.at[d - 1], hr.at[d - 1], dev(source * YZ + me)).wait_recv()

    @pl.loop(1, YZ)
    def _(t):
        g_send(t).start()

    @pl.loop(1, YZ)
    def _(t):
        g_wait(t)

    for d in (2, 1, 3):
        h_send(d).start()
    for d in (1, 3, 2):
        h_wait(d)
    store = pltpu.make_async_copy(full.at[pl.ds(0, TAP_ROWS)], kg, local_sem.at[0])
    store.start()

    @pl.loop(1, YZ)
    def _(t):
        g_send(t).wait_send()

    for d in (1, 3, 2):
        h_send(d).wait_send()
    store.wait()


def upsample(og):
    even = lax.pad(og, jnp.zeros((), BF16), ((0, 0, 0), (0, 9, 1), (0, 0, 0)))
    odd = lax.pad(og, jnp.zeros((), BF16), ((0, 0, 0), (1, 8, 1), (0, 0, 0)))
    before = lax.pad(og[:, 1:], jnp.zeros((), BF16), ((0, 0, 0), (1, 10, 1), (0, 0, 0)))
    return jnp.concatenate([before, even, odd], axis=2)


def on_device(volume, kernel, out_grad):
    v = volume.reshape(2, 6, 2, 24, 256)
    og = upsample(out_grad.reshape(6, 12, 256))
    k = kernel.reshape(9, 3, 256, 256)
    vmem = pl.BlockSpec(memory_space=pltpu.VMEM)
    hbm = pl.BlockSpec(memory_space=pl.ANY)
    dma = pltpu.SemaphoreType.DMA
    out, vg, kg = pl.pallas_call(
        body,
        out_shape=(
            jax.ShapeDtypeStruct((6, 16, 256), BF16),
            jax.ShapeDtypeStruct((2, 6, 2, 24, 256), BF16),
            jax.ShapeDtypeStruct((TAP_ROWS, 256), BF16),
        ),
        in_specs=[vmem, hbm, vmem],
        out_specs=(vmem, vmem, hbm),
        scratch_shapes=[
            pltpu.VMEM((9, 256, 768), BF16),
            pltpu.VMEM((13, 32, 768), BF16),
            pltpu.VMEM((3, 13, 2, 32, 256), BF16),
            pltpu.VMEM((2, 6, 2, 24, 256), BF16),
            pltpu.VMEM((2, 6, 2, 24, 256), BF16),
            pltpu.VMEM((6, 392, 128), F32),
            pltpu.VMEM((3, 12, 2, 32, 256), F32),
            pltpu.VMEM((6, 16, 256), BF16),
            pltpu.VMEM((6, 16, 256), BF16),
            pltpu.VMEM((2, 6, 2, 24, 256), BF16),
            pltpu.VMEM((2, 6, 2, 24, 256), BF16),
            pltpu.VMEM((2, 6, 2, 24, 256), BF16),
            pltpu.VMEM((2, 6, 2, 24, 256), BF16),
            pltpu.VMEM((ROWS, 256), BF16),
            pltpu.VMEM((NX - 1, BLOCK, 256), BF16),
            pltpu.VMEM((BLOCK, 256), BF16),
            pltpu.VMEM((YZ - 1, SHARD, 256), BF16),
            pltpu.VMEM((ROWS, 256), BF16),
            dma((3,)),
            dma((8,)), dma((8,)),
            dma((NX - 1,)), dma((NX - 1,)),
            dma((YZ - 1,)), dma((YZ - 1,)),
            dma((YZ - 1,)), dma((YZ - 1,)),
            dma((NX - 1,)), dma((NX - 1,)),
        ],
        compiler_params=pltpu.CompilerParams(
            collective_id=0, has_side_effects=True, vmem_limit_bytes=56 * 2**20
        ),
    )(v, k, og)
    return (
        out[:, :12].reshape(1, 6, 12, 256),
        vg.reshape(2, 12, 24, 256),
        kg.reshape(3, 3, 3, 256, 256),
    )


def solution(mesh):
    in_specs = (
        P("gz", "af", None, "col"),
        P(None, None, None, "col", "af"),
        P("gz", "col", None, "af"),
    )
    out_specs = (
        P("gz", "col", None, "af"),
        P("gz", "af", None, "col"),
        P(None, None, None, "col", "af"),
    )
    return jax.shard_map(
        on_device, mesh=mesh, in_specs=in_specs, out_specs=out_specs, check_vma=False
    )
```

time: 812 us -> 173 us (0.21); the launches traced: 798 us -> 170 us
  waiting for transfers between devices: 643 us -> 0 us
  Pallas kernels: 0 us -> 156 us
  matrix products: 58.6 us -> 0 us
  local copies, waits for them, and re-layouts: 43.2 us -> 12.5 us
  blocking collectives: 16.2 us -> 0 us
  between operations: 16.8 us -> 0.64 us
  starting transfers between devices: 9.98 us -> 0 us
  other arithmetic: 9.71 us -> 0.73 us
    psum x1 -> x0, waiting for transfers between devices: 619 us -> none  [on_device(): weight_sum = lax.psum(weight_local, 'gz')]
    pallas_call x0 -> x1, Pallas kernels: none -> 156 us  [on_device(): pl.pallas_call(body, out_shape=(jax.ShapeDtypeStruct((6, 16, 256), BF16),...]
    dot_general x81 -> x0, matrix products: 58.6 us -> none  [the longest x27 29 us: on_device(): jnp.einsum('zxyc,zxyf->cf', piece, grad_full, preferred_element_type=jnp....]
    slice x42 -> x1, local copies, waits for them, and re-layouts: 33.1 us -> 0.81 us  [upsample(): og[:, 1:]]
    unnamed x4 -> x0, waiting for transfers between devices: 24.3 us -> none
    all_gather x2 -> x0, blocking collectives: 16.2 us -> none  [the longest x1 14.1 us: on_device(): whole = lax.all_gather(framed, 'af', axis=1, tiled=True)]
    ppermute x2 -> x0, starting transfers between devices: 9.68 us -> none  [from_behind(): lax.ppermute(value, axis, [(source, source + steps) for source in range(i...]
  transfers between devices with their start and end apart: 5 -> 0, of which waited for: 2 -> 0; matrix products, arithmetic and copies ran while one was open for 14% -> 0% of each run, Pallas kernels for 0% -> 0%
where the time goes in v1:
time: 173 us; the launch traced here: 170 us
  Pallas kernels  156 us (90%)
  local copies, waits for them, and re-layouts  12.5 us (7%)
    pallas_call x1, Pallas kernels, on_device(): pl.pallas_call(body, out_shape=(jax.ShapeDtypeStruct((6, 16, 256), BF16),...  156 us
    unnamed x2, local copies, waits for them, and re-layouts  5.87 us

profile of v1, /device:TPU:8, one launch (start us, length us, event | category | flops | bytes accessed | tf_op | source)
XLA Modules:
  0.0 169.9 jit_solution(5558886880465069717)
XLA Ops:
  0.6 0.8 slice.8
  1.4 0.1 pad.9
  1.6 2.2 %pad.11 = bf16[6,32,256]{2,1,0:T(8,128)(2,1)S(1)} pad(bf16[6,12,256]{2,1,0:T(8,128)(2,1)} %bitcast.10, bf16[]{:T(256)} %constant.0.clone.1), padding=0_0_0x1_8_1x0_0_0 | pad | bytes 135170 | tf_op jit(solution)/shard_map/pad | solution.py:270
  3.7 2.2 %pad.10 = bf16[6,32,256]{2,1,0:T(8,128)(2,1)S(1)} pad(bf16[6,12,256]{2,1,0:T(8,128)(2,1)} %bitcast.11, bf16[]{:T(256)} %constant.0.clone.1), padding=0_0_0x0_9_1x0_0_0 | pad | bytes 135170 | tf_op jit(solution)/shard_map/pad | solution.py:269
  5.9 0.7 pad_maximum_fusion.og
  6.6 156.0 %shard_map.58 = (bf16[6,16,256]{2,1,0:T(8,128)(2,1)}, bf16[2,6,2,24,256]{4,3,2,1,0:T(8,128)(2,1)}, bf16[6912,256]{1,0:T(8,128)(2,1)}) custom-call(bf16[2,6,2,24,256]{4,3,2,1,0:T(8,128)(2,1)} %bitcast.12, bf16[9,3,256,256]{3,2,1,0:T(8,128)(2,1)} %bitcast.8, bf16[6,32,768]{2,1,0:T(8,128)(2,1)} %pad_maximum_fusion.og), custom_call_target="tpu_custom_call" | custom-call | tf_op jit(solution)/shard_map/pallas_call | solution.py:282
  162.6 1.4 slice_bitcast_fusion
  164.0 1.7 copy.8
  165.7 4.2 %copy.9 = bf16[3,3,3,256,256]{4,3,2,1,0:T(8,128)(2,1)} copy(bf16[3,3,3,256,256]{4,3,2,1,0:T(8,128)(2,1)} %bitcast.7) | data formatting | bytes 7077888

commit v2 on v1

v2 whole, which is shorter than its diff:
```python
import functools

import jax
import jax.numpy as jnp
from jax import lax
from jax.experimental import pallas as pl
from jax.experimental.pallas import tpu as pltpu
from jax.sharding import PartitionSpec as P

F32 = jnp.float32
BF16 = jnp.bfloat16
MESH = pl.DeviceIdType.MESH
NX, NY, NZ = 4, 2, 8
XY, YZ = NX * NY, NY * NZ
PART_A, PART_B = 64, 48
A_BLOCK, A_PIECE = PART_A * YZ, PART_A * NY
B_BASE, B_BLOCK, B_PIECE = A_BLOCK * NX, PART_B * XY, PART_B * NY
ROWS = B_BASE + B_BLOCK * NZ
TAP_ROWS = 27 * 256
FAR_FIRST = (4, 3, 5, 2, 6, 1, 7, 0)
NEAR_FIRST = (0, 1, 7, 2, 6, 3, 5, 4)


def rows_of(start, size):
    return pl.ds(pl.multiple_of(start, 16), size)


def body(
    v, k, og, out, vg, full,
    k3, up, og3, vs, vin, halo, acc, vacc, oin, osend, vg_af, vg_gz, vin_af, vin_gz,
    ws, rx, s2, ry, br, sb, bx,
    local_sem, es, er, axs, axr, ays, ayr, brs, brr, bxs, bxr,
    gays, gayr, gaxs, gaxr, gbxs, gbxr, gbrs, gbrr,
):
    gz, col, af = lax.axis_index("gz"), lax.axis_index("col"), lax.axis_index("af")
    count = XY * NZ
    x, y, z = gz // YZ, (gz // NZ) % NY, gz % NZ
    upper, lower = lax.rem(gz + 1, count), lax.rem(gz + count - 1, count)

    def dev(g, c=col, a=af):
        return {"gz": g, "col": c, "af": a}

    def at(dx=0, dy=0, dz=0):
        return (lax.rem(x + dx + NX, NX), lax.rem(y + dy + NY, NY), lax.rem(z + dz + NZ, NZ))

    def chip(place):
        return dev((place[0] * NY + place[1]) * NZ + place[2])

    def remote(src, dst, ss, rs, target):
        return pltpu.make_async_remote_copy(
            src_ref=src, dst_ref=dst, send_sem=ss, recv_sem=rs, device_id=target, device_id_type=MESH
        )

    barrier = pltpu.get_barrier_semaphore()

    def greet(target):
        pl.semaphore_signal(barrier, inc=1, device_id=target, device_id_type=MESH)

    greet(dev(gz, c=1 - col))
    greet(dev(gz, a=1 - af))
    for g in (upper, lower):
        greet(dev(g))
        greet(dev(g, a=1 - af))

    @pl.loop(1, YZ)
    def _(t):
        greet(chip(at(0, t % NY, t // NY)))

    @pl.loop(NY, XY)
    def _(t):
        greet(chip(at(t // NY, t % NY, 0)))

    loads = [
        pltpu.make_async_copy(k.at[:, c], k3.at[:, :, pl.ds(c * 256, 256)], local_sem.at[c])
        for c in range(3)
    ]
    for load in loads:
        load.start()

    mine = pl.ds(6 * col, 6)
    up[...] = jnp.zeros(up.shape, F32)
    for i in range(6):
        row = og[i].astype(F32)
        for n in range(2):
            up[n, pl.ds(8 + 32 * i, 12, stride=2)] = row[:, n * 128 : (n + 1) * 128]
    for c in range(3):
        for n in range(2):
            og3[mine, :, pl.ds(c * 256 + n * 128, 128)] = (
                up[n, pl.ds(9 - c, 192)].reshape(6, 32, 128).astype(BF16)
            )
    og3[pl.ds(12, 1)] = jnp.zeros((1, 32, 768), BF16)
    vs[...] = jnp.zeros(vs.shape, BF16)
    ws[pl.ds(TAP_ROWS, ROWS - TAP_ROWS)] = jnp.zeros((ROWS - TAP_ROWS, 256), BF16)
    pl.semaphore_wait(barrier, 1 + 1 + 4 + (YZ - 1) + (XY - NY))

    cot = remote(og3.at[mine], og3.at[mine], es.at[0], er.at[0], dev(gz, c=1 - col))
    to_af = remote(v, vin, es.at[1], er.at[1], dev(gz, a=1 - af))
    top_own = remote(v.at[1], halo.at[0], es.at[2], er.at[2], dev(upper))
    top_other = remote(v.at[1], halo.at[1], es.at[3], er.at[3], dev(upper, a=1 - af))
    for copy in (cot, to_af, top_other, top_own):
        copy.start()

    own_pairs = pl.ds(1 + 6 * af, 6)
    other_pairs = pl.ds(7 - 6 * af, 6)
    for p in range(2):
        vs[p + 1, own_pairs, :, pl.ds(0, 24)] = v[p]

    for load in loads:
        load.wait()
    cot.wait_send()
    other = pl.ds(6 - 6 * col, 6)
    remote(og3.at[other], og3.at[other], es.at[0], er.at[0], dev(gz, c=1 - col)).wait_recv()

    nt = (((1,), (1,)), ((), ()))

    @pl.loop(0, 3)
    def _(a):
        low = og3[pl.ds(0, 12)].reshape(384, 768)
        high = og3[pl.ds(1, 12)].reshape(384, 768)
        even = lax.dot_general(low, k3[a * 3 + 1], nt, preferred_element_type=F32)
        vacc[a, :, 0] = even.reshape(12, 32, 256)
        odd = lax.dot_general(low, k3[a * 3 + 2], nt, preferred_element_type=F32)
        odd = odd + lax.dot_general(high, k3[a * 3], nt, preferred_element_type=F32)
        vacc[a, :, 1] = odd.reshape(12, 32, 256)

    for p in range(2):
        vg_af[p] = vacc[p + 1, pl.ds(6 - 6 * af, 6), :, pl.ds(0, 24)].astype(BF16)
    vg_gz[0] = vacc[0, pl.ds(6 * af, 6), :, pl.ds(0, 24)].astype(BF16)
    vg_gz[1] = vacc[0, pl.ds(6 - 6 * af, 6), :, pl.ds(0, 24)].astype(BF16)
    back_af = remote(vg_af, vin_af, es.at[4], er.at[4], dev(gz, a=1 - af))
    back_own = remote(vg_gz.at[0], vin_gz.at[0], es.at[5], er.at[5], dev(lower))
    back_other = remote(vg_gz.at[1], vin_gz.at[1], es.at[6], er.at[6], dev(lower, a=1 - af))
    for copy in (back_af, back_own, back_other):
        copy.start()

    to_af.wait()
    for p in range(2):
        vs[p + 1, other_pairs, :, pl.ds(0, 24)] = vin[p]
    top_own.wait()
    top_other.wait()
    keep = jnp.where(gz > 0, 1.0, 0.0).astype(BF16)
    vs[0, own_pairs, :, pl.ds(0, 24)] = halo[0] * keep
    vs[0, other_pairs, :, pl.ds(0, 24)] = halo[1] * keep

    def planes(ab):
        b = ab % 3
        return vs[ab // 3, pl.ds(jnp.minimum(b, 1), 12), (b + 1) % 2].reshape(384, 256)

    tn = (((0,), (0,)), ((), ()))

    def weight(ab):
        field = og3[pl.ds(0, 12)].reshape(384, 768)
        grad = lax.dot_general(planes(ab), field, tn, preferred_element_type=F32).astype(BF16)
        for c in range(3):
            ws[rows_of((ab * 3 + c) * 256, 256)] = grad[:, c * 256 : (c + 1) * 256]

    def b_rows(owner, j):
        return rows_of(B_BASE + owner * B_BLOCK + j * B_PIECE, B_PIECE)

    def sign(way):
        return 1 if way == 0 else -1

    def lanes(way):
        return pl.ds(128 * way, 128)

    def ring(way, s, j):
        piece = rows_of(j * B_PIECE, B_PIECE)
        if s == 0:
            src = ws.at[b_rows(at(dz=4)[2], j), lanes(way)]
            dst = br.at[way, 0, piece, lanes(way)]
        else:
            src, dst = br.at[way, s - 1, piece], br.at[way, s, piece]
        return remote(src, dst, brs.at[way, s, j], brr.at[way, s, j], chip(at(dz=sign(way))))

    def near(dj):
        return lax.rem(x + dj, NX)

    def ax_send(d, dz):
        xt, zt = at(dx=d)[0], at(dz=dz)[2]
        return remote(
            ws.at[rows_of(xt * A_BLOCK + zt * A_PIECE, A_PIECE)], rx.at[d - 1, dz],
            axs.at[d - 1, dz], axr.at[d - 1, dz], chip(at(dx=d)),
        )

    def ay_send(dy, dz):
        slot = dz * NY + dy - 1
        yt = at(dy=dy)[1]
        return remote(
            s2.at[dz, rows_of(yt * PART_A, PART_A)], ry.at[slot], ays.at[slot], ayr.at[slot],
            chip(at(dy=dy, dz=dz)),
        )

    def bx_send(dx, dy):
        slot = dx * NY + dy - 1
        xt, yt, _ = at(dx, dy)
        return remote(
            sb.at[rows_of((xt * NY + yt) * PART_B, PART_B)], bx.at[slot], bxs.at[slot], bxr.at[slot],
            chip(at(dx, dy)),
        )

    @pl.loop(0, 4)
    def _(i):
        weight(8 - i)

    @pl.loop(0, NX)
    def _(dj):
        for way in range(2):
            ring(way, 0, near(dj)).start()

    @pl.loop(0, 5)
    def _(i):
        weight(4 - i)

    for dz in FAR_FIRST:
        for d in (2, 1, 3):
            ax_send(d, dz).start()

    acc[...] = jnp.zeros(acc.shape, F32)

    def forward(first):
        @pl.loop(first, first + 3)
        def _(ab):
            term = jnp.dot(planes(ab), k3[ab], preferred_element_type=F32)
            for n in range(6):
                acc[n, pl.ds(8, 384)] += term[:, n * 128 : (n + 1) * 128]

    def ring_step(s):
        @pl.loop(0, NX)
        def _(dj):
            j = near(dj)
            piece = rows_of(j * B_PIECE, B_PIECE)
            for way in range(2):
                ring(way, s, j).wait_recv()
                if s == 3:
                    continue
                own = ws[b_rows(at(dz=sign(way) * (3 - s))[2], j)].astype(F32)
                if s == 0:
                    half, rest = slice(128 * way, 128 * way + 128), slice(128 - 128 * way, 256 - 128 * way)
                    br[way, 0, piece, lanes(way)] = (
                        br[way, 0, piece, lanes(way)].astype(F32) + own[:, half]
                    ).astype(BF16)
                    br[way, 0, piece, lanes(1 - way)] = own[:, rest].astype(BF16)
                else:
                    br[way, s, piece] = (br[way, s, piece].astype(F32) + own).astype(BF16)
                ring(way, s + 1, j).start()
            if s == 3:
                total = ws[b_rows(z, j)].astype(F32)
                total = total + br[0, 3, piece].astype(F32) + br[1, 3, piece].astype(F32)
                sb[piece] = total.astype(BF16)
                bx_send(dj, 1).start()

                @pl.when(dj > 0)
                def _():
                    bx_send(dj, 0).start()

    def a_piece(dz):
        zt = at(dz=dz)[2]
        total = ws[rows_of(x * A_BLOCK + zt * A_PIECE, A_PIECE)].astype(F32)
        for d in range(1, NX):
            ax_send(d, dz).wait_recv()
            total = total + rx[d - 1, dz].astype(F32)
        s2[dz] = total.astype(BF16)
        for dy in range(NY):
            if dy or dz:
                ay_send(dy, dz).start()

    def half(base):
        start = pl.multiple_of(base * 192, 8)
        total = None
        for c in range(3):
            term = jnp.concatenate(
                [
                    acc[c * 2 + lane, pl.ds(7 + c + start, 96, stride=2)]
                    for lane in range(2)
                ],
                axis=1,
            )
            if c == 0:
                place = lax.broadcasted_iota(jnp.int32, (96, 256), 0)
                term = jnp.where(place % 16 == 0, 0.0, term)
            total = term if total is None else total + term
        return total

    across = remote(osend, oin, es.at[7], er.at[7], dev(gz, c=1 - col))
    forward(0)
    for s in range(4):
        ring_step(s)
        if s < 2:
            forward(3 + 3 * s)
        if s == 2:
            osend[...] = half(1 - col).astype(BF16).reshape(6, 16, 256)
            across.start()
        a_piece(FAR_FIRST[2 * s])
        a_piece(FAR_FIRST[2 * s + 1])

    scale = 1.0 / jnp.sqrt(F32(9216))
    total = sb[rows_of((x * NY + y) * PART_B, PART_B)].astype(F32)
    for slot in range(XY - 1):
        bx_send((slot + 1) // NY, (slot + 1) % NY).wait_recv()
        total = total + bx[slot].astype(F32)

    def a_shard(px, py, pz):
        return rows_of(px * A_BLOCK + pz * A_PIECE + py * PART_A, PART_A)

    def b_shard(px, py, pz):
        return rows_of(B_BASE + pz * B_BLOCK + (px * NY + py) * PART_B, PART_B)

    full[b_shard(x, y, z)] = (total * scale).astype(BF16)

    def gbx(dx, dy, source):
        slot = dx * NY + dy - 1
        place = full.at[b_shard(*source)]
        return remote(place, place, gbxs.at[slot], gbxr.at[slot], chip(at(dx, dy)))

    def gay(dy, dz, source):
        slot = dz * NY + dy - 1
        place = full.at[a_shard(*source)]
        return remote(place, place, gays.at[slot], gayr.at[slot], chip(at(dy=dy, dz=dz)))

    @pl.loop(1, XY)
    def _(t):
        gbx(t // NY, t % NY, (x, y, z)).start()

    total = s2[0, rows_of(y * PART_A, PART_A)].astype(F32)
    for dz in FAR_FIRST:
        for dy in range(NY):
            if dy or dz:
                ay_send(dy, dz).wait_recv()
                total = total + ry[dz * NY + dy - 1].astype(F32)
    full[a_shard(x, y, z)] = (total * scale).astype(BF16)

    for dz in NEAR_FIRST:
        for dy in range(NY):
            if dy or dz:
                gay(dy, dz, (x, y, z)).start()

    def gax(d, e, px):
        pz = at(dz=e)[2]
        place = full.at[rows_of(px * A_BLOCK + pz * A_PIECE, A_PIECE)]
        return remote(place, place, gaxs.at[d - 1, e], gaxr.at[d - 1, e], chip(at(dx=d)))

    def gring(way, s, j, arriving=False):
        pz = at(dz=-sign(way) * (s + 1 if arriving else s))[2]
        place = full.at[b_rows(pz, j)] if s < 3 else full.at[b_rows(pz, j), lanes(way)]
        return remote(place, place, gbrs.at[way, s, j], gbrr.at[way, s, j], chip(at(dz=sign(way))))

    def gather_piece(e):
        dz = (NZ - e) % NZ
        for dy in range(NY):
            if dy or dz:
                gay(dy, dz, at(0, -dy, -dz)).wait_recv()
        for d in (2, 1, 3):
            gax(d, e, x).start()

    @pl.loop(0, NX)
    def _(dj):
        j = near(dj)
        back = (NX - dj) % NX
        gbx(back, 1, at(dj, 1, 0)).wait_recv()

        @pl.when(dj > 0)
        def _():
            gbx(back, 0, at(dj, 0, 0)).wait_recv()

        for way in range(2):
            gring(way, 0, j).start()

    gather_piece(NEAR_FIRST[0])

    own_half = half(col)
    oin_copy = remote(osend, oin, es.at[7], er.at[7], dev(gz, c=1 - col))
    oin_copy.wait()
    out[...] = (own_half + oin[...].reshape(96, 256).astype(F32)).astype(BF16).reshape(6, 16, 256)
    back_af.wait()
    back_own.wait()
    back_other.wait()
    own = pl.ds(6 * af, 6)
    vg[0] = (vacc[1, own, :, pl.ds(0, 24)] + vin_af[0].astype(F32)).astype(BF16)
    above = vin_gz[0].astype(F32) + vin_gz[1].astype(F32)
    above = jnp.where(gz < count - 1, above, 0.0)
    vg[1] = (vacc[2, own, :, pl.ds(0, 24)] + vin_af[1].astype(F32) + above).astype(BF16)

    for s in range(4):
        for e in NEAR_FIRST[1 + 2 * s : 3 + 2 * s]:
            gather_piece(e)

        @pl.loop(0, NX)
        def _(dj):
            j = near(dj)
            for way in range(2):
                gring(way, s, j, True).wait_recv()
                if s < 3:
                    gring(way, s + 1, j).start()

    for e in NEAR_FIRST:
        for d in (2, 1, 3):
            gax(d, e, at(dx=-d)[0]).wait_recv()

    @pl.loop(0, NX)
    def _(dj):
        for way in range(2):
            for s in range(4):
                ring(way, s, near(dj)).wait_send()
                gring(way, s, near(dj)).wait_send()

    @pl.loop(0, NZ)
    def _(dz):
        for d in range(1, NX):
            ax_send(d, dz).wait_send()
            gax(d, dz, x).wait_send()

    @pl.loop(1, YZ)
    def _(t):
        ay_send(t % NY, t // NY).wait_send()
        gay(t % NY, t // NY, (x, y, z)).wait_send()

    @pl.loop(1, XY)
    def _(t):
        bx_send(t // NY, t % NY).wait_send()
        gbx(t // NY, t % NY, (x, y, z)).wait_send()


def on_device(volume, kernel, out_grad):
    v = volume.reshape(2, 6, 2, 24, 256)
    og = out_grad.reshape(6, 12, 256)
    k = kernel.reshape(9, 3, 256, 256)
    vmem = pl.BlockSpec(memory_space=pltpu.VMEM)
    hbm = pl.BlockSpec(memory_space=pltpu.HBM)
    dma = pltpu.SemaphoreType.DMA
    planes_shape = (2, 6, 2, 24, 256)

    def pair(*shape):
        return [dma(shape), dma(shape)]

    out, vg, kg = pl.pallas_call(
        body,
        out_shape=(
            jax.ShapeDtypeStruct((6, 16, 256), BF16),
            jax.ShapeDtypeStruct(planes_shape, BF16),
            jax.ShapeDtypeStruct((ROWS, 256), BF16),
        ),
        in_specs=[vmem, hbm, vmem],
        out_specs=(vmem, vmem, vmem),
        scratch_shapes=[
            pltpu.VMEM((9, 256, 768), BF16),
            pltpu.VMEM((2, 208, 128), F32),
            pltpu.VMEM((13, 32, 768), BF16),
            pltpu.VMEM((3, 13, 2, 32, 256), BF16),
            pltpu.VMEM(planes_shape, BF16),
            pltpu.VMEM(planes_shape, BF16),
            pltpu.VMEM((6, 392, 128), F32),
            pltpu.VMEM((3, 12, 2, 32, 256), F32),
            pltpu.VMEM((6, 16, 256), BF16),
            pltpu.VMEM((6, 16, 256), BF16),
            pltpu.VMEM(planes_shape, BF16),
            pltpu.VMEM(planes_shape, BF16),
            pltpu.VMEM(planes_shape, BF16),
            pltpu.VMEM(planes_shape, BF16),
            pltpu.VMEM((ROWS, 256), BF16),
            pltpu.VMEM((NX - 1, NZ, A_PIECE, 256), BF16),
            pltpu.VMEM((NZ, A_PIECE, 256), BF16),
            pltpu.VMEM((YZ - 1, PART_A, 256), BF16),
            pltpu.VMEM((2, 4, B_BLOCK, 256), BF16),
            pltpu.VMEM((B_BLOCK, 256), BF16),
            pltpu.VMEM((XY - 1, PART_B, 256), BF16),
            dma((3,)),
            *pair(8),
            *pair(NX - 1, NZ), *pair(YZ - 1), *pair(2, 4, NX), *pair(XY - 1),
            *pair(YZ - 1), *pair(NX - 1, NZ), *pair(XY - 1), *pair(2, 4, NX),
        ],
        compiler_params=pltpu.CompilerParams(
            collective_id=0, has_side_effects=True, vmem_limit_bytes=40 * 2**20
        ),
    )(v, k, og)
    return (
        out[:, :12].reshape(1, 6, 12, 256),
        vg.reshape(2, 12, 24, 256),
        kg[:TAP_ROWS].reshape(3, 3, 3, 256, 256),
    )


def solution(mesh):
    in_specs = (
        P("gz", "af", None, "col"),
        P(None, None, None, "col", "af"),
        P("gz", "col", None, "af"),
    )
    out_specs = (
        P("gz", "col", None, "af"),
        P("gz", "af", None, "col"),
        P(None, None, None, "col", "af"),
    )
    return jax.shard_map(
        on_device, mesh=mesh, in_specs=in_specs, out_specs=out_specs, check_vma=False
    )
```

time: 173 us -> 103 us (0.60); the launches traced: 170 us -> 102 us
  Pallas kernels: 156 us -> 94.5 us
  local copies, waits for them, and re-layouts: 12.5 us -> 7.11 us
    pallas_call x1, Pallas kernels: 156 us -> 94.5 us  [on_device(): pl.pallas_call(body, out_shape=(jax.ShapeDtypeStruct((6, 16, 256), BF16),...]
    pad x3 -> x0, local copies, waits for them, and re-layouts: 4.44 us -> none  [the longest x1 2.17 us: upsample(): even = lax.pad(og, jnp.zeros((), BF16), ((0, 0, 0), (0, 9, 1), (0, 0, 0)))]
    unnamed x2 -> x7, local copies, waits for them, and re-layouts: 5.87 us -> 4.47 us
where the time goes in v2:
time: 103 us; the launch traced here: 102 us
  Pallas kernels  94.5 us (92%)
  local copies, waits for them, and re-layouts  7.11 us (7%)
    pallas_call x1, Pallas kernels, on_device(): pl.pallas_call(body, out_shape=(jax.ShapeDtypeStruct((6, 16, 256), BF16),...  94.5 us
    unnamed x7, local copies, waits for them, and re-layouts  4.47 us

profile of v2, /device:TPU:8, one launch (start us, length us, event | category | flops | bytes accessed | tf_op | source)
XLA Modules:
  0.0 102.2 jit_solution(8229205530923766368)
XLA Ops:
  0.6 0.0 copy-start
  0.6 2.0 %copy-done = bf16[3,3,3,256,256]{4,3,2,1,0:T(8,128)(2,1)S(1)} copy-done((bf16[3,3,3,256,256]{4,3,2,1,0:T(8,128)(2,1)S(1)}, bf16[3,3,3,256,256]{4,3,2,1,0:T(8,128)(2,1)}, u32[]{:S(2)}) %copy-start) | copy-done | bytes 3538968
  2.6 0.0 copy-start.1
  2.6 1.0 copy-done.1
  3.6 0.0 copy-start.2
  3.6 0.8 copy-done.2
  4.4 94.5 %shard_map.58 = (bf16[6,16,256]{2,1,0:T(8,128)(2,1)S(1)}, bf16[2,6,2,24,256]{4,3,2,1,0:T(8,128)(2,1)S(1)}, bf16[7168,256]{1,0:T(8,128)(2,1)S(1)}) custom-call(bf16[2,6,2,24,256]{4,3,2,1,0:T(8,128)(2,1)S(1)} %bitcast.9, bf16[9,3,256,256]{3,2,1,0:T(8,128)(2,1)S(1)} %bitcast.7, bf16[6,12,256]{2,1,0:T(8,128)(2,1)S(1)} %bitcast.10), custom_call_target="tpu_custom_call" | custom-call | tf_op jit(solution)/shard_map/pallas_call | solution.py:435
  98.9 0.6 slice_bitcast_fusion
  99.5 2.0 %slice.7 = bf16[6912,256]{1,0:T(8,128)(2,1)} slice(bf16[7168,256]{1,0:T(8,128)(2,1)S(1)} %get-tuple-element.8), slice={[0:6912], [0:256]} | slice | bytes 7077888 | tf_op jit(solution)/shard_map/slice | solution.py:478
  101.5 0.7 copy.7
Async XLA Ops:
  0.6 2.0 %copy-start = (bf16[3,3,3,256,256]{4,3,2,1,0:T(8,128)(2,1)S(1)}, bf16[3,3,3,256,256]{4,3,2,1,0:T(8,128)(2,1)}, u32[]{:S(2)}) copy-start(bf16[3,3,3,256,256]{4,3,2,1,0:T(8,128)(2,1)} %param.4) | copy-start | bytes 10616836
  2.6 1.0 copy-start.1
  3.6 0.8 copy-start.2

commit v3 on v2

--- a/solution.py
+++ b/solution.py
@@ -14,9 +14,11 @@
 XY, YZ = NX * NY, NY * NZ
 PART_A, PART_B = 64, 48
 A_BLOCK, A_PIECE = PART_A * YZ, PART_A * NY
-B_BASE, B_BLOCK, B_PIECE = A_BLOCK * NX, PART_B * XY, PART_B * NY
-ROWS = B_BASE + B_BLOCK * NZ
-TAP_ROWS = 27 * 256
+B_BLOCK, B_PIECE = PART_B * XY, PART_B * NY
+B_CHUNK = B_PIECE * NZ
+A_BASE = B_BLOCK * NZ
+ROWS = A_BASE + A_BLOCK * NX
+FIRST_TAP = 256
 FAR_FIRST = (4, 3, 5, 2, 6, 1, 7, 0)
 NEAR_FIRST = (0, 1, 7, 2, 6, 3, 5, 4)
 
@@ -26,11 +28,11 @@
 
 
 def body(
-    v, k, og, out, vg, full,
-    k3, up, og3, vs, vin, halo, acc, vacc, oin, osend, vg_af, vg_gz, vin_af, vin_gz,
+    v_hbm, k, og_hbm, out, vg, full,
+    v, og, k3, up, og3, vs, vin, halo, acc, vacc, oin, osend, vg_af, vg_gz, vin_af, vin_gz,
     ws, rx, s2, ry, br, sb, bx,
     local_sem, es, er, axs, axr, ays, ayr, brs, brr, bxs, bxr,
-    gays, gayr, gaxs, gaxr, gbxs, gbxr, gbrs, gbrr,
+    gazs, gazr, gaxs, gaxr, gbxs, gbxr, gbrs, gbrr,
 ):
     gz, col, af = lax.axis_index("gz"), lax.axis_index("col"), lax.axis_index("af")
     count = XY * NZ
@@ -74,11 +76,18 @@
         pltpu.make_async_copy(k.at[:, c], k3.at[:, :, pl.ds(c * 256, 256)], local_sem.at[c])
         for c in range(3)
     ]
+    load_og = pltpu.make_async_copy(og_hbm, og, local_sem.at[3])
+    load_v = pltpu.make_async_copy(v_hbm, v, local_sem.at[4])
+    load_og.start()
+    load_v.start()
     for load in loads:
         load.start()
 
     mine = pl.ds(6 * col, 6)
     up[...] = jnp.zeros(up.shape, F32)
+    vs[...] = jnp.zeros(vs.shape, BF16)
+    ws[pl.ds(0, FIRST_TAP)] = jnp.zeros((FIRST_TAP, 256), BF16)
+    load_og.wait()
     for i in range(6):
         row = og[i].astype(F32)
         for n in range(2):
@@ -89,15 +98,16 @@
                 up[n, pl.ds(9 - c, 192)].reshape(6, 32, 128).astype(BF16)
             )
     og3[pl.ds(12, 1)] = jnp.zeros((1, 32, 768), BF16)
-    vs[...] = jnp.zeros(vs.shape, BF16)
-    ws[pl.ds(TAP_ROWS, ROWS - TAP_ROWS)] = jnp.zeros((ROWS - TAP_ROWS, 256), BF16)
+    load_v.wait()
     pl.semaphore_wait(barrier, 1 + 1 + 4 + (YZ - 1) + (XY - NY))
 
     cot = remote(og3.at[mine], og3.at[mine], es.at[0], er.at[0], dev(gz, c=1 - col))
-    to_af = remote(v, vin, es.at[1], er.at[1], dev(gz, a=1 - af))
-    top_own = remote(v.at[1], halo.at[0], es.at[2], er.at[2], dev(upper))
+    to_af = [
+        remote(v.at[p], vin.at[p], es.at[p + 1], er.at[p + 1], dev(gz, a=1 - af)) for p in range(2)
+    ]
+    top_own = remote(v.at[1], halo.at[0], es.at[8], er.at[8], dev(upper))
     top_other = remote(v.at[1], halo.at[1], es.at[3], er.at[3], dev(upper, a=1 - af))
-    for copy in (cot, to_af, top_other, top_own):
+    for copy in (cot, to_af[1], top_own, to_af[0], top_other):
         copy.start()
 
     own_pairs = pl.ds(1 + 6 * af, 6)
@@ -123,6 +133,112 @@
         odd = odd + lax.dot_general(high, k3[a * 3], nt, preferred_element_type=F32)
         vacc[a, :, 1] = odd.reshape(12, 32, 256)
 
+    def planes(ab):
+        b = ab % 3
+        return vs[ab // 3, pl.ds(jnp.minimum(b, 1), 12), (b + 1) % 2].reshape(384, 256)
+
+    tn = (((0,), (0,)), ((), ()))
+
+    def weight(ab):
+        field = og3[pl.ds(0, 12)].reshape(384, 768)
+        grad = lax.dot_general(planes(ab), field, tn, preferred_element_type=F32).astype(BF16)
+        for c in range(3):
+            ws[rows_of(FIRST_TAP + (ab * 3 + c) * 256, 256)] = grad[:, c * 256 : (c + 1) * 256]
+
+    def b_rows(owner, j):
+        return rows_of(j * B_CHUNK + owner * B_PIECE, B_PIECE)
+
+    def sign(way):
+        return 1 if way == 0 else -1
+
+    def lanes(way):
+        return pl.ds(128 * way, 128)
+
+    def ring(way, s, j):
+        piece = rows_of(j * B_PIECE, B_PIECE)
+        if s == 0:
+            src = ws.at[b_rows(at(dz=4)[2], j), lanes(way)]
+            dst = br.at[way, 0, piece, lanes(way)]
+        else:
+            src, dst = br.at[way, s - 1, piece], br.at[way, s, piece]
+        return remote(src, dst, brs.at[way, s, j], brr.at[way, s, j], chip(at(dz=sign(way))))
+
+    def near(dj):
+        return lax.rem(x + dj, NX)
+
+    def ax_send(d, dz):
+        xt, zt = at(dx=d)[0], at(dz=dz)[2]
+        return remote(
+            ws.at[rows_of(A_BASE + xt * A_BLOCK + zt * A_PIECE, A_PIECE)], rx.at[d - 1, dz],
+            axs.at[d - 1, dz], axr.at[d - 1, dz], chip(at(dx=d)),
+        )
+
+    def ay_send(dy, dz):
+        slot = dz * NY + dy - 1
+        yt = at(dy=dy)[1]
+        return remote(
+            s2.at[dz, rows_of(yt * PART_A, PART_A)], ry.at[slot], ays.at[slot], ayr.at[slot],
+            chip(at(dy=dy, dz=dz)),
+        )
+
+    def bx_send(dx, dy):
+        slot = dx * NY + dy - 1
+        xt, yt, _ = at(dx, dy)
+        return remote(
+            sb.at[rows_of((xt * NY + yt) * PART_B, PART_B)], bx.at[slot], bxs.at[slot], bxr.at[slot],
+            chip(at(dx, dy)),
+        )
+
+    to_af[1].wait()
+    vs[2, other_pairs, :, pl.ds(0, 24)] = vin[1]
+
+    acc[...] = jnp.zeros(acc.shape, F32)
+
+    def forward(first):
+        @pl.loop(first, first + 3)
+        def _(ab):
+            term = jnp.dot(planes(ab), k3[ab], preferred_element_type=F32)
+            for n in range(6):
+                acc[n, pl.ds(8, 384)] += term[:, n * 128 : (n + 1) * 128]
+
+    def enter(j):
+        for way in range(2):
+            ring(way, 0, j).start()
+
+    def leave(xt):
+        @pl.when(x != xt)
+        def _():
+            for dz in FAR_FIRST:
+                ax_send(lax.rem(xt - x + NX, NX), dz).start()
+
+    weight(8)
+    weight(7)
+    leave(3)
+    weight(6)
+    leave(2)
+    forward(6)
+    to_af[0].wait()
+    vs[1, other_pairs, :, pl.ds(0, 24)] = vin[0]
+    weight(5)
+    leave(1)
+    weight(4)
+    weight(3)
+    leave(0)
+    forward(3)
+    top_own.wait()
+    top_other.wait()
+    keep = jnp.where(gz > 0, 1.0, 0.0).astype(BF16)
+    vs[0, own_pairs, :, pl.ds(0, 24)] = halo[0] * keep
+    vs[0, other_pairs, :, pl.ds(0, 24)] = halo[1] * keep
+
+    weight(2)
+    enter(3)
+    weight(1)
+    enter(2)
+    weight(0)
+    enter(1)
+    enter(0)
+
     for p in range(2):
         vg_af[p] = vacc[p + 1, pl.ds(6 - 6 * af, 6), :, pl.ds(0, 24)].astype(BF16)
     vg_gz[0] = vacc[0, pl.ds(6 * af, 6), :, pl.ds(0, 24)].astype(BF16)
@@ -133,101 +249,11 @@
     for copy in (back_af, back_own, back_other):
         copy.start()
 
-    to_af.wait()
-    for p in range(2):
-        vs[p + 1, other_pairs, :, pl.ds(0, 24)] = vin[p]
-    top_own.wait()
-    top_other.wait()
-    keep = jnp.where(gz > 0, 1.0, 0.0).astype(BF16)
-    vs[0, own_pairs, :, pl.ds(0, 24)] = halo[0] * keep
-    vs[0, other_pairs, :, pl.ds(0, 24)] = halo[1] * keep
-
-    def planes(ab):
-        b = ab % 3
-        return vs[ab // 3, pl.ds(jnp.minimum(b, 1), 12), (b + 1) % 2].reshape(384, 256)
-
-    tn = (((0,), (0,)), ((), ()))
-
-    def weight(ab):
-        field = og3[pl.ds(0, 12)].reshape(384, 768)
-        grad = lax.dot_general(planes(ab), field, tn, preferred_element_type=F32).astype(BF16)
-        for c in range(3):
-            ws[rows_of((ab * 3 + c) * 256, 256)] = grad[:, c * 256 : (c + 1) * 256]
-
-    def b_rows(owner, j):
-        return rows_of(B_BASE + owner * B_BLOCK + j * B_PIECE, B_PIECE)
-
-    def sign(way):
-        return 1 if way == 0 else -1
-
-    def lanes(way):
-        return pl.ds(128 * way, 128)
-
-    def ring(way, s, j):
-        piece = rows_of(j * B_PIECE, B_PIECE)
-        if s == 0:
-            src = ws.at[b_rows(at(dz=4)[2], j), lanes(way)]
-            dst = br.at[way, 0, piece, lanes(way)]
-        else:
-            src, dst = br.at[way, s - 1, piece], br.at[way, s, piece]
-        return remote(src, dst, brs.at[way, s, j], brr.at[way, s, j], chip(at(dz=sign(way))))
-
-    def near(dj):
-        return lax.rem(x + dj, NX)
-
-    def ax_send(d, dz):
-        xt, zt = at(dx=d)[0], at(dz=dz)[2]
-        return remote(
-            ws.at[rows_of(xt * A_BLOCK + zt * A_PIECE, A_PIECE)], rx.at[d - 1, dz],
-            axs.at[d - 1, dz], axr.at[d - 1, dz], chip(at(dx=d)),
-        )
-
-    def ay_send(dy, dz):
-        slot = dz * NY + dy - 1
-        yt = at(dy=dy)[1]
-        return remote(
-            s2.at[dz, rows_of(yt * PART_A, PART_A)], ry.at[slot], ays.at[slot], ayr.at[slot],
-            chip(at(dy=dy, dz=dz)),
-        )
-
-    def bx_send(dx, dy):
-        slot = dx * NY + dy - 1
-        xt, yt, _ = at(dx, dy)
-        return remote(
-            sb.at[rows_of((xt * NY + yt) * PART_B, PART_B)], bx.at[slot], bxs.at[slot], bxr.at[slot],
-            chip(at(dx, dy)),
-        )
-
-    @pl.loop(0, 4)
-    def _(i):
-        weight(8 - i)
-
-    @pl.loop(0, NX)
-    def _(dj):
-        for way in range(2):
-            ring(way, 0, near(dj)).start()
-
-    @pl.loop(0, 5)
-    def _(i):
-        weight(4 - i)
-
-    for dz in FAR_FIRST:
-        for d in (2, 1, 3):
-            ax_send(d, dz).start()
-
-    acc[...] = jnp.zeros(acc.shape, F32)
-
-    def forward(first):
-        @pl.loop(first, first + 3)
-        def _(ab):
-            term = jnp.dot(planes(ab), k3[ab], preferred_element_type=F32)
-            for n in range(6):
-                acc[n, pl.ds(8, 384)] += term[:, n * 128 : (n + 1) * 128]
-
-    def ring_step(s):
-        @pl.loop(0, NX)
-        def _(dj):
-            j = near(dj)
+    def ring_step(s, first=0, last=NX):
+        @pl.loop(first, last)
+        def _(n):
+            j = NX - 1 - n
+            dx = lax.rem(j - x + NX, NX)
             piece = rows_of(j * B_PIECE, B_PIECE)
             for way in range(2):
                 ring(way, s, j).wait_recv()
@@ -247,15 +273,15 @@
                 total = ws[b_rows(z, j)].astype(F32)
                 total = total + br[0, 3, piece].astype(F32) + br[1, 3, piece].astype(F32)
                 sb[piece] = total.astype(BF16)
-                bx_send(dj, 1).start()
-
-                @pl.when(dj > 0)
+                bx_send(dx, 1).start()
+
+                @pl.when(dx > 0)
                 def _():
-                    bx_send(dj, 0).start()
+                    bx_send(dx, 0).start()
 
     def a_piece(dz):
         zt = at(dz=dz)[2]
-        total = ws[rows_of(x * A_BLOCK + zt * A_PIECE, A_PIECE)].astype(F32)
+        total = ws[rows_of(A_BASE + x * A_BLOCK + zt * A_PIECE, A_PIECE)].astype(F32)
         for d in range(1, NX):
             ax_send(d, dz).wait_recv()
             total = total + rx[d - 1, dz].astype(F32)
@@ -282,16 +308,37 @@
         return total
 
     across = remote(osend, oin, es.at[7], er.at[7], dev(gz, c=1 - col))
+    def finish_output():
+        own_half = half(col)
+        across.wait()
+        out[...] = (own_half + oin[...].reshape(96, 256).astype(F32)).astype(BF16).reshape(6, 16, 256)
+
+    def finish_gradient():
+        back_af.wait()
+        back_own.wait()
+        back_other.wait()
+        own = pl.ds(6 * af, 6)
+        vg[0] = (vacc[1, own, :, pl.ds(0, 24)] + vin_af[0].astype(F32)).astype(BF16)
+        above = vin_gz[0].astype(F32) + vin_gz[1].astype(F32)
+        above = jnp.where(gz < count - 1, above, 0.0)
+        vg[1] = (vacc[2, own, :, pl.ds(0, 24)] + vin_af[1].astype(F32) + above).astype(BF16)
+
     forward(0)
-    for s in range(4):
-        ring_step(s)
-        if s < 2:
-            forward(3 + 3 * s)
-        if s == 2:
-            osend[...] = half(1 - col).astype(BF16).reshape(6, 16, 256)
-            across.start()
-        a_piece(FAR_FIRST[2 * s])
-        a_piece(FAR_FIRST[2 * s + 1])
+    osend[...] = half(1 - col).astype(BF16).reshape(6, 16, 256)
+    across.start()
+    a_piece(FAR_FIRST[0])
+    ring_step(0)
+    a_piece(FAR_FIRST[1])
+    ring_step(1)
+    a_piece(FAR_FIRST[2])
+    a_piece(FAR_FIRST[3])
+    ring_step(2)
+    a_piece(FAR_FIRST[4])
+    a_piece(FAR_FIRST[5])
+    ring_step(3)
+    finish_output()
+    a_piece(FAR_FIRST[6])
+    a_piece(FAR_FIRST[7])
 
     scale = 1.0 / jnp.sqrt(F32(9216))
     total = sb[rows_of((x * NY + y) * PART_B, PART_B)].astype(F32)
@@ -300,10 +347,10 @@
         total = total + bx[slot].astype(F32)
 
     def a_shard(px, py, pz):
-        return rows_of(px * A_BLOCK + pz * A_PIECE + py * PART_A, PART_A)
+        return rows_of(A_BASE + px * A_BLOCK + pz * A_PIECE + py * PART_A, PART_A)
 
     def b_shard(px, py, pz):
-        return rows_of(B_BASE + pz * B_BLOCK + (px * NY + py) * PART_B, PART_B)
+        return rows_of(px * B_CHUNK + pz * B_PIECE + py * PART_B, PART_B)
 
     full[b_shard(x, y, z)] = (total * scale).astype(BF16)
 
@@ -312,10 +359,9 @@
         place = full.at[b_shard(*source)]
         return remote(place, place, gbxs.at[slot], gbxr.at[slot], chip(at(dx, dy)))
 
-    def gay(dy, dz, source):
-        slot = dz * NY + dy - 1
+    def gaz(dz, source):
         place = full.at[a_shard(*source)]
-        return remote(place, place, gays.at[slot], gayr.at[slot], chip(at(dy=dy, dz=dz)))
+        return remote(place, place, gazs.at[dz - 1], gazr.at[dz - 1], chip(at(dz=dz)))
 
     @pl.loop(1, XY)
     def _(t):
@@ -329,15 +375,14 @@
                 total = total + ry[dz * NY + dy - 1].astype(F32)
     full[a_shard(x, y, z)] = (total * scale).astype(BF16)
 
-    for dz in NEAR_FIRST:
-        for dy in range(NY):
-            if dy or dz:
-                gay(dy, dz, (x, y, z)).start()
-
-    def gax(d, e, px):
-        pz = at(dz=e)[2]
-        place = full.at[rows_of(px * A_BLOCK + pz * A_PIECE, A_PIECE)]
-        return remote(place, place, gaxs.at[d - 1, e], gaxr.at[d - 1, e], chip(at(dx=d)))
+    for dz in NEAR_FIRST[1:]:
+        gaz(dz, (x, y, z)).start()
+
+    def gax(t, e, arriving=False):
+        dx, dy = t // NY, t % NY
+        source = at(-dx, -dy, e) if arriving else (x, y, at(dz=e)[2])
+        place = full.at[a_shard(*source)]
+        return remote(place, place, gaxs.at[t - 1, e], gaxr.at[t - 1, e], chip(at(dx, dy)))
 
     def gring(way, s, j, arriving=False):
         pz = at(dz=-sign(way) * (s + 1 if arriving else s))[2]
@@ -345,12 +390,14 @@
         return remote(place, place, gbrs.at[way, s, j], gbrr.at[way, s, j], chip(at(dz=sign(way))))
 
     def gather_piece(e):
-        dz = (NZ - e) % NZ
-        for dy in range(NY):
-            if dy or dz:
-                gay(dy, dz, at(0, -dy, -dz)).wait_recv()
-        for d in (2, 1, 3):
-            gax(d, e, x).start()
+        if e:
+            dz = NZ - e
+            gaz(dz, at(dz=-dz)).wait_recv()
+        for t in (4, 5, 2, 3, 6, 7, 1):
+            gax(t, e).start()
+
+    gather_piece(NEAR_FIRST[0])
+    finish_gradient()
 
     @pl.loop(0, NX)
     def _(dj):
@@ -364,21 +411,6 @@
 
         for way in range(2):
             gring(way, 0, j).start()
-
-    gather_piece(NEAR_FIRST[0])
-
-    own_half = half(col)
-    oin_copy = remote(osend, oin, es.at[7], er.at[7], dev(gz, c=1 - col))
-    oin_copy.wait()
-    out[...] = (own_half + oin[...].reshape(96, 256).astype(F32)).astype(BF16).reshape(6, 16, 256)
-    back_af.wait()
-    back_own.wait()
-    back_other.wait()
-    own = pl.ds(6 * af, 6)
-    vg[0] = (vacc[1, own, :, pl.ds(0, 24)] + vin_af[0].astype(F32)).astype(BF16)
-    above = vin_gz[0].astype(F32) + vin_gz[1].astype(F32)
-    above = jnp.where(gz < count - 1, above, 0.0)
-    vg[1] = (vacc[2, own, :, pl.ds(0, 24)] + vin_af[1].astype(F32) + above).astype(BF16)
 
     for s in range(4):
         for e in NEAR_FIRST[1 + 2 * s : 3 + 2 * s]:
@@ -392,9 +424,10 @@
                 if s < 3:
                     gring(way, s + 1, j).start()
 
-    for e in NEAR_FIRST:
-        for d in (2, 1, 3):
-            gax(d, e, at(dx=-d)[0]).wait_recv()
+    @pl.loop(0, NZ)
+    def _(e):
+        for t in range(1, XY):
+            gax(t, e, True).wait_recv()
 
     @pl.loop(0, NX)
     def _(dj):
@@ -407,12 +440,16 @@
     def _(dz):
         for d in range(1, NX):
             ax_send(d, dz).wait_send()
-            gax(d, dz, x).wait_send()
+        for t in range(1, XY):
+            gax(t, dz).wait_send()
 
     @pl.loop(1, YZ)
     def _(t):
         ay_send(t % NY, t // NY).wait_send()
-        gay(t % NY, t // NY, (x, y, z)).wait_send()
+
+    @pl.loop(1, NZ)
+    def _(dz):
+        gaz(dz, (x, y, z)).wait_send()
 
     @pl.loop(1, XY)
     def _(t):
@@ -439,9 +476,11 @@
             jax.ShapeDtypeStruct(planes_shape, BF16),
             jax.ShapeDtypeStruct((ROWS, 256), BF16),
         ),
-        in_specs=[vmem, hbm, vmem],
+        in_specs=[hbm, hbm, hbm],
         out_specs=(vmem, vmem, vmem),
         scratch_shapes=[
+            pltpu.VMEM(planes_shape, BF16),
+            pltpu.VMEM((6, 12, 256), BF16),
             pltpu.VMEM((9, 256, 768), BF16),
             pltpu.VMEM((2, 208, 128), F32),
             pltpu.VMEM((13, 32, 768), BF16),
@@ -463,19 +502,19 @@
             pltpu.VMEM((2, 4, B_BLOCK, 256), BF16),
             pltpu.VMEM((B_BLOCK, 256), BF16),
             pltpu.VMEM((XY - 1, PART_B, 256), BF16),
-            dma((3,)),
-            *pair(8),
+            dma((5,)),
+            *pair(9),
             *pair(NX - 1, NZ), *pair(YZ - 1), *pair(2, 4, NX), *pair(XY - 1),
-            *pair(YZ - 1), *pair(NX - 1, NZ), *pair(XY - 1), *pair(2, 4, NX),
+            *pair(NZ - 1), *pair(XY - 1, NZ), *pair(XY - 1), *pair(2, 4, NX),
         ],
         compiler_params=pltpu.CompilerParams(
             collective_id=0, has_side_effects=True, vmem_limit_bytes=40 * 2**20
         ),
-    )(v, k, og)
+    )(*(pltpu.with_memory_space_constraint(a, pltpu.HBM) for a in (v, k, og)))
     return (
         out[:, :12].reshape(1, 6, 12, 256),
         vg.reshape(2, 12, 24, 256),
-        kg[:TAP_ROWS].reshape(3, 3, 3, 256, 256),
+        kg[FIRST_TAP:].reshape(3, 3, 3, 256, 256),
     )
 
 

time: 103 us -> 98.3 us (0.954)
  local copies, waits for them, and re-layouts: 7.11 us -> 3.36 us
    unnamed x7 -> x1, local copies, waits for them, and re-layouts: 4.47 us -> 0.71 us
where the time goes in v3:
time: 98.3 us; the launch traced here: 97.7 us
  Pallas kernels  93.7 us (95%)
  local copies, waits for them, and re-layouts  3.36 us (3%)
    pallas_call x1, Pallas kernels, on_device(): pl.pallas_call(body, out_shape=(jax.ShapeDtypeStruct((6, 16, 256), BF16),...  93.7 us
    slice x1, local copies, waits for them, and re-layouts, on_device(): kg[FIRST_TAP:].reshape(3, 3, 3, 256, 256)  2.02 us

profile of v3, /device:TPU:8, one launch (start us, length us, event | category | flops | bytes accessed | tf_op | source)
XLA Modules:
  0.0 97.7 jit_solution(10091338714174888038)
XLA Ops:
  0.6 93.7 %shard_map.58 = (bf16[6,16,256]{2,1,0:T(8,128)(2,1)S(1)}, bf16[2,6,2,24,256]{4,3,2,1,0:T(8,128)(2,1)S(1)}, bf16[7168,256]{1,0:T(8,128)(2,1)S(1)}) custom-call(bf16[2,6,2,24,256]{4,3,2,1,0:T(8,128)(2,1)} %bitcast.10, bf16[9,3,256,256]{3,2,1,0:T(8,128)(2,1)} %bitcast.9, bf16[6,12,256]{2,1,0:T(8,128)(2,1)} %bitcast.11), custom_call_target="tpu_custom_call" | custom-call | tf_op jit(solution)/shard_map/pallas_call | solution.py:472
  94.4 0.6 slice_bitcast_fusion
  95.0 2.0 %slice.7 = bf16[6912,256]{1,0:T(8,128)(2,1)} slice(bf16[7168,256]{1,0:T(8,128)(2,1)S(1)} %get-tuple-element.8), slice={[256:7168], [0:256]} | slice | bytes 7077888 | tf_op jit(solution)/shard_map/slice | solution.py:517
  97.0 0.7 copy.7

commit v4 on v3

--- a/solution.py
+++ b/solution.py
@@ -30,8 +30,8 @@
 def body(
     v_hbm, k, og_hbm, out, vg, full,
     v, og, k3, up, og3, vs, vin, halo, acc, vacc, oin, osend, vg_af, vg_gz, vin_af, vin_gz,
-    ws, rx, s2, ry, br, sb, bx,
-    local_sem, es, er, axs, axr, ays, ayr, brs, brr, bxs, bxr,
+    ws, rx, s2, ry, s3, rz, br, sb, bx,
+    local_sem, es, er, axs, axr, ays, ayr, azs, azr, brs, brr, bxs, bxr,
     gazs, gazr, gaxs, gaxr, gbxs, gbxr, gbrs, gbrr,
 ):
     gz, col, af = lax.axis_index("gz"), lax.axis_index("col"), lax.axis_index("af")
@@ -64,11 +64,11 @@
         greet(dev(g))
         greet(dev(g, a=1 - af))
 
-    @pl.loop(1, YZ)
-    def _(t):
-        greet(chip(at(0, t % NY, t // NY)))
-
-    @pl.loop(NY, XY)
+    @pl.loop(1, NZ)
+    def _(dz):
+        greet(chip(at(dz=dz)))
+
+    @pl.loop(1, XY)
     def _(t):
         greet(chip(at(t // NY, t % NY, 0)))
 
@@ -99,7 +99,7 @@
             )
     og3[pl.ds(12, 1)] = jnp.zeros((1, 32, 768), BF16)
     load_v.wait()
-    pl.semaphore_wait(barrier, 1 + 1 + 4 + (YZ - 1) + (XY - NY))
+    pl.semaphore_wait(barrier, 1 + 1 + 4 + (NZ - 1) + (XY - 1))
 
     cot = remote(og3.at[mine], og3.at[mine], es.at[0], er.at[0], dev(gz, c=1 - col))
     to_af = [
@@ -107,7 +107,7 @@
     ]
     top_own = remote(v.at[1], halo.at[0], es.at[8], er.at[8], dev(upper))
     top_other = remote(v.at[1], halo.at[1], es.at[3], er.at[3], dev(upper, a=1 - af))
-    for copy in (cot, to_af[1], top_own, to_af[0], top_other):
+    for copy in (cot, to_af[1], top_own):
         copy.start()
 
     own_pairs = pl.ds(1 + 6 * af, 6)
@@ -123,8 +123,7 @@
 
     nt = (((1,), (1,)), ((), ()))
 
-    @pl.loop(0, 3)
-    def _(a):
+    def backward(a):
         low = og3[pl.ds(0, 12)].reshape(384, 768)
         high = og3[pl.ds(1, 12)].reshape(384, 768)
         even = lax.dot_general(low, k3[a * 3 + 1], nt, preferred_element_type=F32)
@@ -132,6 +131,14 @@
         odd = lax.dot_general(low, k3[a * 3 + 2], nt, preferred_element_type=F32)
         odd = odd + lax.dot_general(high, k3[a * 3], nt, preferred_element_type=F32)
         vacc[a, :, 1] = odd.reshape(12, 32, 256)
+
+    @pl.loop(0, 2)
+    def _(a):
+        backward(a)
+
+    to_af[1].wait_send()
+    to_af[0].start()
+    backward(2)
 
     def planes(ab):
         b = ab % 3
@@ -173,13 +180,14 @@
             axs.at[d - 1, dz], axr.at[d - 1, dz], chip(at(dx=d)),
         )
 
-    def ay_send(dy, dz):
-        slot = dz * NY + dy - 1
-        yt = at(dy=dy)[1]
+    def ay_send(dz):
+        yt = at(dy=1)[1]
         return remote(
-            s2.at[dz, rows_of(yt * PART_A, PART_A)], ry.at[slot], ays.at[slot], ayr.at[slot],
-            chip(at(dy=dy, dz=dz)),
+            s2.at[dz, rows_of(yt * PART_A, PART_A)], ry.at[dz], ays.at[dz], ayr.at[dz], chip(at(dy=1))
         )
+
+    def az_send(dz):
+        return remote(s3.at[dz], rz.at[dz - 1], azs.at[dz - 1], azr.at[dz - 1], chip(at(dz=dz)))
 
     def bx_send(dx, dy):
         slot = dx * NY + dy - 1
@@ -189,7 +197,7 @@
             chip(at(dx, dy)),
         )
 
-    to_af[1].wait()
+    to_af[1].wait_recv()
     vs[2, other_pairs, :, pl.ds(0, 24)] = vin[1]
 
     acc[...] = jnp.zeros(acc.shape, F32)
@@ -216,8 +224,10 @@
     leave(3)
     weight(6)
     leave(2)
+    to_af[0].wait_send()
+    top_other.start()
     forward(6)
-    to_af[0].wait()
+    to_af[0].wait_recv()
     vs[1, other_pairs, :, pl.ds(0, 24)] = vin[0]
     weight(5)
     leave(1)
@@ -286,9 +296,14 @@
             ax_send(d, dz).wait_recv()
             total = total + rx[d - 1, dz].astype(F32)
         s2[dz] = total.astype(BF16)
-        for dy in range(NY):
-            if dy or dz:
-                ay_send(dy, dz).start()
+        ay_send(dz).start()
+
+    def a_pass(dz):
+        ay_send(dz).wait_recv()
+        total = s2[dz, rows_of(y * PART_A, PART_A)].astype(F32) + ry[dz].astype(F32)
+        s3[dz] = total.astype(BF16)
+        if dz:
+            az_send(dz).start()
 
     def half(base):
         start = pl.multiple_of(base * 192, 8)
@@ -332,13 +347,21 @@
     ring_step(1)
     a_piece(FAR_FIRST[2])
     a_piece(FAR_FIRST[3])
+    a_pass(FAR_FIRST[0])
     ring_step(2)
     a_piece(FAR_FIRST[4])
+    a_pass(FAR_FIRST[1])
     a_piece(FAR_FIRST[5])
+    a_pass(FAR_FIRST[2])
     ring_step(3)
     finish_output()
     a_piece(FAR_FIRST[6])
+    a_pass(FAR_FIRST[3])
     a_piece(FAR_FIRST[7])
+    a_pass(FAR_FIRST[4])
+    a_pass(FAR_FIRST[5])
+    a_pass(FAR_FIRST[6])
+    a_pass(FAR_FIRST[7])
 
     scale = 1.0 / jnp.sqrt(F32(9216))
     total = sb[rows_of((x * NY + y) * PART_B, PART_B)].astype(F32)
@@ -367,12 +390,10 @@
     def _(t):
         gbx(t // NY, t % NY, (x, y, z)).start()
 
-    total = s2[0, rows_of(y * PART_A, PART_A)].astype(F32)
-    for dz in FAR_FIRST:
-        for dy in range(NY):
-            if dy or dz:
-                ay_send(dy, dz).wait_recv()
-                total = total + ry[dz * NY + dy - 1].astype(F32)
+    total = s3[0].astype(F32)
+    for dz in FAR_FIRST[:-1]:
+        az_send(dz).wait_recv()
+        total = total + rz[dz - 1].astype(F32)
     full[a_shard(x, y, z)] = (total * scale).astype(BF16)
 
     for dz in NEAR_FIRST[1:]:
@@ -398,6 +419,29 @@
 
     gather_piece(NEAR_FIRST[0])
     finish_gradient()
+
+    @pl.loop(0, NX)
+    def _(dj):
+        for way in range(2):
+            for s in range(4):
+                ring(way, s, near(dj)).wait_send()
+
+    @pl.loop(0, NZ)
+    def _(dz):
+        for d in range(1, NX):
+            ax_send(d, dz).wait_send()
+
+    @pl.loop(0, NZ)
+    def _(dz):
+        ay_send(dz).wait_send()
+
+    @pl.loop(1, NZ)
+    def _(dz):
+        az_send(dz).wait_send()
+
+    @pl.loop(1, XY)
+    def _(t):
+        bx_send(t // NY, t % NY).wait_send()
 
     @pl.loop(0, NX)
     def _(dj):
@@ -428,24 +472,13 @@
     def _(e):
         for t in range(1, XY):
             gax(t, e, True).wait_recv()
+            gax(t, e).wait_send()
 
     @pl.loop(0, NX)
     def _(dj):
         for way in range(2):
             for s in range(4):
-                ring(way, s, near(dj)).wait_send()
                 gring(way, s, near(dj)).wait_send()
-
-    @pl.loop(0, NZ)
-    def _(dz):
-        for d in range(1, NX):
-            ax_send(d, dz).wait_send()
-        for t in range(1, XY):
-            gax(t, dz).wait_send()
-
-    @pl.loop(1, YZ)
-    def _(t):
-        ay_send(t % NY, t // NY).wait_send()
 
     @pl.loop(1, NZ)
     def _(dz):
@@ -453,7 +486,6 @@
 
     @pl.loop(1, XY)
     def _(t):
-        bx_send(t // NY, t % NY).wait_send()
         gbx(t // NY, t % NY, (x, y, z)).wait_send()
 
 
@@ -498,13 +530,15 @@
             pltpu.VMEM((ROWS, 256), BF16),
             pltpu.VMEM((NX - 1, NZ, A_PIECE, 256), BF16),
             pltpu.VMEM((NZ, A_PIECE, 256), BF16),
-            pltpu.VMEM((YZ - 1, PART_A, 256), BF16),
+            pltpu.VMEM((NZ, PART_A, 256), BF16),
+            pltpu.VMEM((NZ, PART_A, 256), BF16),
+            pltpu.VMEM((NZ - 1, PART_A, 256), BF16),
             pltpu.VMEM((2, 4, B_BLOCK, 256), BF16),
             pltpu.VMEM((B_BLOCK, 256), BF16),
             pltpu.VMEM((XY - 1, PART_B, 256), BF16),
             dma((5,)),
             *pair(9),
-            *pair(NX - 1, NZ), *pair(YZ - 1), *pair(2, 4, NX), *pair(XY - 1),
+            *pair(NX - 1, NZ), *pair(NZ), *pair(NZ - 1), *pair(2, 4, NX), *pair(XY - 1),
             *pair(NZ - 1), *pair(XY - 1, NZ), *pair(XY - 1), *pair(2, 4, NX),
         ],
         compiler_params=pltpu.CompilerParams(

time: 98.3 us -> 90.7 us (0.923)
  Pallas kernels: 93.7 us -> 86.6 us
    pallas_call x1, Pallas kernels: 93.7 us -> 86.6 us  [on_device(): pl.pallas_call(body, out_shape=(jax.ShapeDtypeStruct((6, 16, 256), BF16),...]
where the time goes in v4:
time: 90.7 us; the launch traced here: 90.6 us
  Pallas kernels  86.6 us (95%)
  local copies, waits for them, and re-layouts  3.36 us (4%)
    pallas_call x1, Pallas kernels, on_device(): pl.pallas_call(body, out_shape=(jax.ShapeDtypeStruct((6, 16, 256), BF16),...  86.6 us
    slice x1, local copies, waits for them, and re-layouts, on_device(): kg[FIRST_TAP:].reshape(3, 3, 3, 256, 256)  2.02 us

profile of v4, /device:TPU:8, one launch (start us, length us, event | category | flops | bytes accessed | tf_op | source)
XLA Modules:
  0.0 90.6 jit_solution(3244658495640452488)
XLA Ops:
  0.6 86.6 %shard_map.58 = (bf16[6,16,256]{2,1,0:T(8,128)(2,1)S(1)}, bf16[2,6,2,24,256]{4,3,2,1,0:T(8,128)(2,1)S(1)}, bf16[7168,256]{1,0:T(8,128)(2,1)S(1)}) custom-call(bf16[2,6,2,24,256]{4,3,2,1,0:T(8,128)(2,1)} %bitcast.10, bf16[9,3,256,256]{3,2,1,0:T(8,128)(2,1)} %bitcast.9, bf16[6,12,256]{2,1,0:T(8,128)(2,1)} %bitcast.11), custom_call_target="tpu_custom_call" | custom-call | tf_op jit(solution)/shard_map/pallas_call | solution.py:504
  87.2 0.6 slice_bitcast_fusion
  87.9 2.0 %slice.7 = bf16[6912,256]{1,0:T(8,128)(2,1)} slice(bf16[7168,256]{1,0:T(8,128)(2,1)S(1)} %get-tuple-element.8), slice={[256:7168], [0:256]} | slice | bytes 7077888 | tf_op jit(solution)/shard_map/slice | solution.py:551
  89.9 0.7 copy.7

commit v5 on v4

--- a/solution.py
+++ b/solution.py
@@ -457,7 +457,7 @@
             gring(way, 0, j).start()
 
     for s in range(4):
-        for e in NEAR_FIRST[1 + 2 * s : 3 + 2 * s]:
+        for e in NEAR_FIRST[(1, 4, 7, 8)[s] : (4, 7, 8, 8)[s]]:
             gather_piece(e)
 
         @pl.loop(0, NX)

time: 90.7 us -> 90.3 us (level)
  Pallas kernels: 86.6 us -> 85.6 us
    pallas_call x1, Pallas kernels: 86.6 us -> 85.6 us  [on_device(): pl.pallas_call(body, out_shape=(jax.ShapeDtypeStruct((6, 16, 256), BF16),...]
where the time goes in v5:
time: 90.3 us; the launch traced here: 89.6 us
  Pallas kernels  85.6 us (95%)
  local copies, waits for them, and re-layouts  3.36 us (4%)
    pallas_call x1, Pallas kernels, on_device(): pl.pallas_call(body, out_shape=(jax.ShapeDtypeStruct((6, 16, 256), BF16),...  85.6 us
    slice x1, local copies, waits for them, and re-layouts, on_device(): kg[FIRST_TAP:].reshape(3, 3, 3, 256, 256)  2.02 us

profile of v5, /device:TPU:8, one launch (start us, length us, event | category | flops | bytes accessed | tf_op | source)
XLA Modules:
  0.0 89.6 jit_solution(185325757334768149)
XLA Ops:
  0.6 85.6 %shard_map.58 = (bf16[6,16,256]{2,1,0:T(8,128)(2,1)S(1)}, bf16[2,6,2,24,256]{4,3,2,1,0:T(8,128)(2,1)S(1)}, bf16[7168,256]{1,0:T(8,128)(2,1)S(1)}) custom-call(bf16[2,6,2,24,256]{4,3,2,1,0:T(8,128)(2,1)} %bitcast.10, bf16[9,3,256,256]{3,2,1,0:T(8,128)(2,1)} %bitcast.9, bf16[6,12,256]{2,1,0:T(8,128)(2,1)} %bitcast.11), custom_call_target="tpu_custom_call" | custom-call | tf_op jit(solution)/shard_map/pallas_call | solution.py:504
  86.3 0.6 slice_bitcast_fusion
  86.9 2.0 %slice.7 = bf16[6912,256]{1,0:T(8,128)(2,1)} slice(bf16[7168,256]{1,0:T(8,128)(2,1)S(1)} %get-tuple-element.8), slice={[256:7168], [0:256]} | slice | bytes 7077888 | tf_op jit(solution)/shard_map/slice | solution.py:551
  88.9 0.7 copy.7
